TPU v7x, 256 devices: a whole 4x4x8 slice. The times are simulated.
256 devices in a mesh: ta: 8 (over z_lo, core), col: 32 (over x, y, z_hi).
Axes of the slice: x: 4, y: 4, z: 8 (z_hi: 2, z_lo: 4; z = z_hi * 4 + z_lo), core: 2. Of those that a mesh axis runs over, the one named last changes fastest.
Arguments:
- voltages: bfloat16 [2048, 1024, 128], P('ta', 'col'), may hold values from -6 to 6
- taps_filter: float32 [16, 128], replicated, may hold values from -0.125 to 0.125
Outputs:
- spectra: bfloat16 [64, 2, 2048, 1024], P('col', None, 'ta')
- visibilities: float32 [1024, 64, 2, 1024], P('ta', 'col')
All inputs are finite; a program needn't handle non-finite values.
Results may differ from a plain program's by a relative error of at most 0.015.
Values may be sent and summed in bfloat16 or wider, within the bound.
A program may use at most 128 MiB of HBM per device.

v0:
```python
import jax
import jax.numpy as jnp
from jax import lax
from jax.sharding import PartitionSpec as P


def from_behind(x, axis, by):
    count = lax.axis_size(axis)
    pairs = [(i, i + by) for i in range(count) if 0 <= i + by < count]
    return lax.ppermute(x, axis, pairs)


def make_table(width, chans):
    samples = jnp.arange(width, dtype=jnp.int32)
    freqs = jnp.arange(chans, dtype=jnp.int32)
    phase = (samples[:, None] * freqs[None, :] % width).astype(jnp.float32)
    angle = 2.0 * jnp.pi * phase / width
    return jnp.concatenate([jnp.cos(angle), -jnp.sin(angle)], axis=1).astype(jnp.bfloat16)


def block_gram(left, right, scale):
    product = jnp.einsum("cksr,cjsm->ckrjm", left, right, preferred_element_type=jnp.float32)
    real_part = product[:, 0, :, 0] + product[:, 1, :, 1]
    imag_part = product[:, 0, :, 1] - product[:, 1, :, 0]
    return jnp.transpose(jnp.stack([real_part, imag_part], axis=2), (1, 0, 2, 3)) * scale


def body(voltages, taps_filter):
    frames, local_in, width = voltages.shape
    chans = width // 2
    history = taps_filter.shape[0] - 1
    before = from_behind(voltages[frames - history :], "ta", 1)
    padded = jnp.concatenate([before, voltages], axis=0).astype(jnp.float32)
    total = jnp.zeros((frames, local_in, width), jnp.float32)
    for tap in range(history + 1):
        total = total + taps_filter[tap][None, None, :] * padded[tap : tap + frames]
    filtered = total.astype(jnp.bfloat16)
    table = make_table(width, chans)
    spec = jnp.dot(
        filtered.reshape(frames * local_in, width), table, preferred_element_type=jnp.float32
    )
    spec = spec.astype(jnp.bfloat16).reshape(frames, local_in, 2, chans)
    spec = jnp.transpose(spec, (3, 2, 0, 1))
    turned = lax.all_to_all(spec, "col", split_axis=0, concat_axis=3, tiled=True)
    groups = lax.axis_size("ta")
    scale = 1.0 / (frames * groups)
    visib = lax.psum_scatter(
        block_gram(turned, turned, scale).astype(jnp.bfloat16),
        "ta",
        scatter_dimension=0,
        tiled=True,
    ).astype(jnp.float32)
    return (turned, visib)


def solution(mesh):
    placed = (P("ta", "col", None), P())
    return jax.shard_map(
        body,
        mesh=mesh,
        in_specs=placed,
        out_specs=(P("col", None, "ta", None), P("ta", "col", None, None)),
        check_vma=False,
    )
```

profile of v0, /device:TPU:33, one launch (start us, length us, event | category | flops | bytes accessed | tf_op | source)
XLA Modules:
  0.0 254.9 jit_solution(11587126038669517500)
XLA Ops:
  7.2 0.0 reduce-scatter.2.cloned.1.call-start
  7.2 0.9 slice.112
  8.1 4.1 %collective-permute-start = (bf16[15,32,128]{2,1,0:T(8,128)(2,1)S(1)}, bf16[15,32,128]{2,1,0:T(8,128)(2,1)S(1)}, u32[]{:S(2)}, u32[]{:S(2)}) collective-permute-start(bf16[15,32,128]{2,1,0:T(8,128)(2,1)S(1)} %slice.112), channel_id=1, source_target_pairs={{0,32},{32,64},{64,96},{96,128},{128,160},{160,192},{192,224},{1,3... | collective-permute-start | bytes 368648 | tf_op jit(solution)/shard_map/ppermute | solution.py:10
  12.2 1.0 slice_bitcast_fusion.17
  13.3 0.2 negate_convert_fusion
  13.4 0.7 collective-permute-done
  14.1 1.9 maximum_convert_fusion
  16.0 8.9 %fusion.6 = bf16[256,32,128]{2,1,0:T(8,128)(2,1)S(1)} fusion(f32[271,32,128]{2,1,0:T(8,128)S(1)} %maximum_convert_fusion, f32[128]{0:T(128)S(1)} %get-tuple-element.24, f32[128]{0:T(128)S(1)} %get-tuple-element.25, f32[128]{0:T(128)S(1)} %get-tuple-element.11, f32[128]{0:T(128)S(1)} %get-tuple-element.12, f32[128]{0:T(128)S(1)} %get-tuple-element.13, ...), kind=kLoop, calls=%fused_computation.12 | loop fusion | flops 33554432 | bytes 69214208 | tf_op jit(solution)/shard_map/convert_element_type | solution.py:37
  24.9 2.0 convolution_convert_fusion
  26.9 8.2 %reshape.63 = bf16[256,32,2,64]{3,2,1,0:T(2,128)(2,1)} reshape(bf16[8192,128]{1,0:T(8,128)(2,1)} %convolution_convert_fusion) | data formatting | bytes 4194304 | tf_op jit(solution)/shard_map/reshape | solution.py:42
  35.1 7.5 %copy.23 = bf16[64,2,256,32]{2,3,1,0:T(8,128)(2,1)S(1)} copy(bf16[64,2,256,32]{0,1,3,2:T(2,128)(2,1)} %bitcast.67) | data formatting | bytes 4194304 | tf_op jit(solution)/shard_map/transpose | solution.py:43
  42.7 67.3 %all_to_all.18 = bf16[64,2,256,32]{2,3,1,0:T(8,128)(2,1)S(1)} all-to-all(bf16[64,2,256,32]{2,3,1,0:T(8,128)(2,1)S(1)} %copy.23), channel_id=1, replica_groups=mesh['ta'=8,'col'=32] {'col'}, dimensions={0} | all-to-all | bytes 4194304 | tf_op jit(solution)/shard_map/all_to_all | solution.py:44
  110.0 0.2 copy.24
  110.2 13.1 %fusion.31 = f32[2,2,1024,2,1024]{4,2,3,1,0:T(8,128)} fusion(bf16[2,2,256,1024,1]{2,3,4,1,0:T(8,128)(2,1)S(1)} %bitcast.64, bf16[2,2,256,1024,1]{2,3,1,4,0:T(8,128)(2,1)S(1)} %bitcast.65), kind=kOutput, calls=%fused_computation.74 | convolution fusion | flops 4294967296 | bytes 37748736 | tf_op jit(solution)/shard_map/cksr,cjsm->ckrjm/dot_general | solution.py:22
  123.3 12.2 %fusion.2 = f32[2,1024,1,1024]{3,1,0,2:T(8,128)} fusion(f32[2,2,1024,2,1024]{4,2,3,1,0:T(8,128)} %fusion.31), kind=kLoop, calls=%fused_computation.5 | loop fusion | flops 2097152 | bytes 25165824 | tf_op jit(solution)/shard_map/sub | solution.py:24
  135.5 12.0 %fusion.4 = f32[2,1024,1,1024]{3,1,0,2:T(8,128)} fusion(f32[2,2,1024,2,1024]{4,2,3,1,0:T(8,128)} %fusion.31), kind=kLoop, calls=%fused_computation.8 | loop fusion | flops 2097152 | bytes 25165824 | tf_op jit(solution)/shard_map/add | solution.py:23
  147.4 9.7 %fusion.1 = bf16[1024,2,2,1024]{3,0,1,2:T(8,128)(2,1)} fusion(f32[2,1024,1,1024]{3,1,0,2:T(8,128)} %fusion.2, f32[2,1024,1,1024]{3,1,0,2:T(8,128)} %fusion.4), kind=kLoop, calls=%fused_computation.3 | loop fusion | flops 12582912 | bytes 25165824 | tf_op jit(solution)/shard_map/convert_element_type | solution.py:48
  157.1 0.0 reduce-scatter.2.cloned.1.call-update
  157.1 2.4 copy.28
  159.5 84.9 %reduce-scatter.2.cloned.1.call-done = bf16[128,2,2,1024]{3,0,1,2:T(8,128)(2,1)} async-done(((bf16[1024,2,2,1024]{3,0,1,2:T(8,128)(2,1)}), bf16[128,2,2,1024]{3,0,1,2:T(8,128)(2,1)}) %reduce-scatter.2.cloned.1.call-update) | async-done | bytes 1048592 | tf_op jit(solution)/shard_map/reduce_scatter | solution.py:47
  244.4 3.6 %copy.29 = f32[128,2,2,1024]{3,2,1,0:T(2,128)} copy(bf16[128,2,2,1024]{3,0,1,2:T(8,128)(2,1)} %reduce-scatter.2.cloned.1.call-done) | data formatting | bytes 3145728
Async XLA Ops:
  7.2 237.3 %reduce-scatter.2.cloned.1.call-start = ((), (), s32[]{:S(2)}) async-start(), calls=%async_computation.2 | async-start | bytes 9437184 | tf_op jit(solution)/shard_map/reduce_scatter | solution.py:47
  8.1 6.0 %collective-permute-start = (bf16[15,32,128]{2,1,0:T(8,128)(2,1)S(1)}, bf16[15,32,128]{2,1,0:T(8,128)(2,1)S(1)}, u32[]{:S(2)}, u32[]{:S(2)}) collective-permute-start(bf16[15,32,128]{2,1,0:T(8,128)(2,1)S(1)} %slice.112), channel_id=1, source_target_pairs={{0,32},{32,64},{64,96},{96,128},{128,160},{160,192},{192,224},{1,3... | collective-permute-start | bytes 368648 | tf_op jit(solution)/shard_map/ppermute | solution.py:10
Sparse Core Ops, SparseCore 0:
  157.3 87.1 reduce-scatter.1
where the time goes:
time: 258 us; the launch traced here: 255 us
  waiting for transfers between devices  85.6 us (33%)
  blocking collectives  67.3 us (26%)
  other arithmetic  44.8 us (17%)
  local copies, waits for them, and re-layouts  23.9 us (9%)
  matrix products  15.1 us (6%)
  between operations  14.1 us (5%)
  starting transfers between devices  4.14 us (2%)
    reduce_scatter x1, waiting for transfers between devices, body(): lax.psum_scatter(block_gram(turned, turned, scale).astype(jnp.bfloat16),...  84.9 us
    all_to_all x1, blocking collectives, body(): lax.all_to_all(spec, 'col', split_axis=0, concat_axis=3, tiled=True)  67.3 us
    dot_general x1, matrix products, block_gram(): jnp.einsum('cksr,cjsm->ckrjm', left, right, preferred_element_type=jnp.fl...  13.1 us
    sub x1, other arithmetic, block_gram(): imag_part = product[:, 0, :, 1] - product[:, 1, :, 0]  12.2 us
    add x1, other arithmetic, block_gram(): real_part = product[:, 0, :, 0] + product[:, 1, :, 1]  12 us
    convert_element_type x1, other arithmetic, body(): block_gram(turned, turned, scale).astype(jnp.bfloat16)  9.69 us
    convert_element_type x1, other arithmetic, body(): filtered = total.astype(jnp.bfloat16)  8.92 us
    reshape x1, local copies, waits for them, and re-layouts, body(): spec = spec.astype(jnp.bfloat16).reshape(frames, local_in, 2, chans)  8.21 us
  transfers between devices with their start and end apart: 2, of which 2 were waited for; matrix products, arithmetic and copies ran while one was open for 1% of the time, Pallas kernels for 0%

commit v1 on v0

v1 whole, which is shorter than its diff:
```python
import jax
import jax.numpy as jnp
import numpy as np
from jax import lax
from jax.experimental import pallas as pl
from jax.experimental.pallas import tpu as pltpu
from jax.sharding import PartitionSpec as P

MESH = pl.DeviceIdType.MESH
F32 = jnp.float32
BF16 = jnp.bfloat16

TAPS = 16
FR = 128
FRAMES = 256
LOCAL = 32
COLS = 32
NIN = 1024
CHIPS = 4
BLK = NIN // CHIPS
QF = FRAMES // 4
JC = 16
NJC = QF // JC
GROUPS = COLS // 4

ORDER = [(i, j) for j in range(CHIPS - 1, -1, -1) for i in range(j + 1)]


def make_table_rows():
    samples = np.arange(FR)
    chans = np.arange(FR // 2)
    angle = 2.0 * np.pi * ((chans[:, None] * samples[None, :]) % FR) / FR
    both = np.stack([np.cos(angle), -np.sin(angle)], axis=1)
    return jnp.asarray(both.reshape(FR, FR), F32).astype(BF16)


def make_regroup():
    perm = np.zeros((4, 4, LOCAL, 4, 4, LOCAL), np.float32)
    for i in range(4):
        for b in range(4):
            for n in range(LOCAL):
                perm[i, b, n, b, i, n] = 1.0
    return jnp.asarray(perm.reshape(512, 512), BF16)


def kernel(
    volt, taps, table, regroup, spec_out, vis_out,
    padded, filt, wide, sendbuf, recvbuf, spec, gram, turned, part, outgo_a, outgo_b, from_out, from_in, halves, halves_in,
    load_sem, halo_sem, a2a_send, a2a_recv, own_sem, pair_sem, line_send, line_recv, half_sem, out_sem,
):
    ta = lax.axis_index("ta")
    col = lax.axis_index("col")
    chip = ta // 2
    core = ta % 2
    mirror = chip // 2
    middle = chip * (1 - mirror) + (3 - chip) * mirror
    inner = {"ta": (chip + 1 - 2 * mirror) * 2 + core, "col": col}
    outer = {"ta": (chip - 1 + 2 * mirror) * 2 + core, "col": col}
    sibling = {"ta": chip * 2 + 1 - core, "col": col}
    before = {"ta": ta - 1, "col": col}
    after = {"ta": ta + 1, "col": col}
    is_end = middle == 0
    is_middle = middle == 1
    cross_after = jnp.logical_and(core == 1, chip < CHIPS - 1)
    cross_before = jnp.logical_and(core == 0, chip > 0)

    load = pltpu.make_async_copy(volt, padded.at[pl.ds(TAPS, FRAMES)], load_sem.at[0])
    load.start()

    barrier = pltpu.get_barrier_semaphore()

    def greet(device):
        pl.semaphore_signal(barrier, inc=1, device_id=device, device_id_type=MESH)

    def greet_col(step, carry):
        greet({"ta": ta, "col": (col + step) % COLS})
        return carry

    lax.fori_loop(1, COLS, greet_col, 0)
    greet(sibling)
    greet(inner)

    @pl.when(is_middle)
    def _():
        greet(outer)

    @pl.when(cross_after)
    def _():
        greet(after)

    @pl.when(cross_before)
    def _():
        greet(before)

    @pl.when(ta == 0)
    def _():
        padded[0:TAPS] = jnp.zeros((TAPS, LOCAL, FR), BF16)

    load.wait()

    def front(chunk):
        def filter_part(step, carry):
            group = step // 2
            rows = pl.ds(pl.multiple_of((step % 2) * 16, 16), 16)
            out_rows = pl.ds(pl.multiple_of(group * LOCAL + (step % 2) * 16, 16), 16)
            weights = [taps[t : t + 1, :] for t in range(TAPS)]
            for part_of in range(JC // 8):
                base = group * QF + chunk * JC + part_of * 8 + 1
                held = [padded[base + i, rows, :].astype(F32) for i in range(TAPS + 7)]
                for o in range(8):
                    total = weights[0] * held[o]
                    for t in range(1, TAPS):
                        total = total + weights[t] * held[o + t]
                    filt[part_of * 8 + o, out_rows, :] = total.astype(BF16)
            return carry

        lax.fori_loop(0, 8, filter_part, 0)
        for j in range(JC):
            wide[pl.ds(j, FR, stride=JC), :] = lax.dot_general(
                table[...], filt[j], (((1,), (1,)), ((), ())), preferred_element_type=F32
            )
        sendbuf[:, pl.ds(chunk * JC, JC), :] = wide[...].reshape(FR, JC, FR).astype(BF16)

    def send_chunk(chunk):
        rows = pl.ds(chunk * JC, JC)

        def send_one(step, carry):
            peer = (col + step) % COLS
            pltpu.make_async_remote_copy(
                src_ref=sendbuf.at[pl.ds(peer * 4, 4), rows],
                dst_ref=recvbuf.at[col, :, rows],
                send_sem=a2a_send.at[peer],
                recv_sem=a2a_recv.at[col],
                device_id={"ta": ta, "col": peer},
                device_id_type=MESH,
            ).start()
            return carry

        lax.fori_loop(1, COLS, send_one, 0)

    halo = pltpu.make_async_remote_copy(
        src_ref=padded.at[pl.ds(FRAMES, TAPS)],
        dst_ref=padded.at[pl.ds(0, TAPS)],
        send_sem=halo_sem.at[0],
        recv_sem=halo_sem.at[1],
        device_id=after,
        device_id_type=MESH,
    )

    front(1)
    pl.semaphore_wait(
        barrier,
        COLS + 1 + middle + cross_after.astype(jnp.int32) + cross_before.astype(jnp.int32),
    )

    @pl.when(ta < 2 * CHIPS - 1)
    def _():
        halo.start()

    send_chunk(1)
    front(2)
    send_chunk(2)
    front(3)
    send_chunk(3)

    @pl.when(ta > 0)
    def _():
        halo.wait_recv()

    front(0)
    send_chunk(0)
    own = pltpu.make_async_copy(sendbuf.at[pl.ds(col * 4, 4)], recvbuf.at[col], own_sem.at[0])
    own.start()
    own.wait()

    def regroup_one(g, carry):
        lanes = pl.ds(pl.multiple_of(g * 128, 128), 128)
        for i in range(4):
            source = g * 4 + i

            @pl.when(source != col)
            def _():
                pltpu.make_async_remote_copy(
                    src_ref=recvbuf.at[source],
                    dst_ref=recvbuf.at[source],
                    send_sem=a2a_send.at[source],
                    recv_sem=a2a_recv.at[source],
                    device_id={"ta": ta, "col": source},
                    device_id_type=MESH,
                ).wait_recv()

        total = jnp.zeros((4 * QF, 512), F32)
        for i in range(4):
            total = total + jnp.dot(
                recvbuf[g * 4 + i].reshape(4 * QF, FR),
                regroup[i * 128 : (i + 1) * 128, :],
                preferred_element_type=F32,
            )
        for b in range(4):
            spec[:, b * QF : (b + 1) * QF, lanes] = (
                total[:, b * 128 : (b + 1) * 128].astype(BF16).reshape(4, QF, 128)
            )
        pltpu.make_async_remote_copy(
            src_ref=spec.at[pl.ds(2 * (1 - core), 2), :, lanes],
            dst_ref=gram.at[:, :, lanes],
            send_sem=pair_sem.at[0],
            recv_sem=pair_sem.at[1],
            device_id=sibling,
            device_id_type=MESH,
        ).start()
        return carry

    lax.fori_loop(0, GROUPS, regroup_one, 0)
    write_spec = pltpu.make_async_copy(spec, spec_out, out_sem.at[0])
    write_spec.start()
    pair = pltpu.make_async_remote_copy(
        src_ref=spec.at[pl.ds(2 * (1 - core), 2)],
        dst_ref=gram,
        send_sem=pair_sem.at[0],
        recv_sem=pair_sem.at[1],
        device_id=sibling,
        device_id_type=MESH,
    )
    pair.wait_recv()

    def actual(i, j):
        return i + mirror * (3 - i - j), j + mirror * (3 - i - j)

    def planes_of(i, j):
        return 1 if i == j else 2

    def slot_of(i, j):
        rows, columns = actual(i, j)
        return rows * CHIPS + columns

    def stream(buffer, landing, i, j, channel, device):
        slot = slot_of(i, j)
        planes = pl.ds(0, planes_of(i, j))
        return pltpu.make_async_remote_copy(
            src_ref=buffer.at[slot, planes],
            dst_ref=landing.at[slot, planes],
            send_sem=line_send.at[channel, slot],
            recv_sem=line_recv.at[channel, slot],
            device_id=device,
            device_id_type=MESH,
        )

    own_real = 2 * core
    turned[0:256, :] = spec[own_real + 1]
    turned[256:512, :] = -spec[own_real]
    turned[512:768, :] = gram[1]
    turned[768:1024, :] = -gram[0]

    row_id = lax.broadcasted_iota(jnp.int32, (BLK, BLK), 0)
    col_id = lax.broadcasted_iota(jnp.int32, (BLK, BLK), 1)

    for i, j in ORDER:
        rows, columns = actual(i, j)
        left = pl.ds(pl.multiple_of(rows * BLK, BLK), BLK)
        right = pl.ds(pl.multiple_of(columns * BLK, BLK), BLK)
        slot = slot_of(i, j)
        lhs = jnp.concatenate(
            [spec[own_real, :, left], spec[own_real + 1, :, left], gram[0, :, left], gram[1, :, left]], axis=0
        )
        rhs = jnp.concatenate(
            [spec[own_real, :, right], spec[own_real + 1, :, right], gram[0, :, right], gram[1, :, right]], axis=0
        )
        dims = (((0,), (0,)), ((), ()))
        real = lax.dot_general(lhs, rhs, dims, preferred_element_type=F32)
        imag = lax.dot_general(lhs, turned[:, right], dims, preferred_element_type=F32)
        if i == j:
            part[slot, 0] = jnp.where(row_id <= col_id, real, imag)
        else:
            part[slot, 0] = real
            part[slot, 1] = imag
        if j >= 1:

            @pl.when(is_end)
            def _():
                for plane in range(planes_of(i, j)):
                    outgo_a[slot, plane] = part[slot, plane].astype(BF16)
                stream(outgo_a, from_out, i, j, 0, inner).start()

    inward = [(i, j) for i, j in ORDER if j >= 2]
    outward = [(0, j) for j in range(CHIPS - 1, -1, -1)]

    @pl.when(is_middle)
    def _():
        for step in range(len(inward)):
            i, j = inward[step]
            slot = slot_of(i, j)
            stream(outgo_a, from_out, i, j, 0, outer).wait_recv()
            for plane in range(planes_of(i, j)):
                outgo_a[slot, plane] = (part[slot, plane] + from_out[slot, plane].astype(F32)).astype(BF16)
            stream(outgo_a, from_in, i, j, 1, inner).start()
            if step < len(outward):
                i, j = outward[step]
                slot = slot_of(i, j)
                stream(outgo_b, from_in, i, j, 1, inner).wait_recv()
                for plane in range(planes_of(i, j)):
                    outgo_b[slot, plane] = (part[slot, plane] + from_in[slot, plane].astype(F32)).astype(BF16)
                stream(outgo_b, from_in, i, j, 2, outer).start()

    scale = 1.0 / (FRAMES * 2 * CHIPS)

    def finish(i, j, own_is_row, total):
        rows, columns = actual(i, j)
        if i == j:
            lanes = pl.ds(pl.multiple_of(rows * BLK, BLK), BLK)
            packed = total(0)
            flipped = packed.T
            real = jnp.where(row_id <= col_id, packed, flipped)
            imag = jnp.where(row_id > col_id, packed, jnp.where(row_id == col_id, 0.0, -flipped))
            for h in range(2):
                halves[h, 0, :, lanes] = real[h * 128 : (h + 1) * 128] * scale
                halves[h, 1, :, lanes] = imag[h * 128 : (h + 1) * 128] * scale
        else:
            straight = mirror == (0 if own_is_row else 1)

            @pl.when(straight)
            def _():
                lanes = pl.ds(pl.multiple_of(columns * BLK, BLK), BLK)
                for plane in range(2):
                    value = total(plane) * scale
                    for h in range(2):
                        halves[h, plane, :, lanes] = value[h * 128 : (h + 1) * 128]

            @pl.when(jnp.logical_not(straight))
            def _():
                lanes = pl.ds(pl.multiple_of(rows * BLK, BLK), BLK)
                for plane in range(2):
                    value = total(plane).T * (scale if plane == 0 else -scale)
                    for h in range(2):
                        halves[h, plane, :, lanes] = value[h * 128 : (h + 1) * 128]

    @pl.when(is_end)
    def _():
        for i, j in outward:
            slot = slot_of(i, j)
            stream(outgo_b, from_in, i, j, 2, inner).wait_recv()
            finish(i, j, True, lambda plane: part[slot, plane] + from_in[slot, plane].astype(F32))

    @pl.when(is_middle)
    def _():
        for i, j in [(1, 3), (1, 2), (0, 1), (1, 1)]:
            slot = slot_of(i, j)
            if j == 1:
                stream(outgo_a, from_out, i, j, 0, outer).wait_recv()
            if i == 1:
                stream(outgo_a, from_in, i, j, 1, inner).wait_recv()
            finish(
                i, j, i == 1,
                lambda plane: part[slot, plane] + from_out[slot, plane].astype(F32) + from_in[slot, plane].astype(F32),
            )

    swap = pltpu.make_async_remote_copy(
        src_ref=halves.at[1 - core],
        dst_ref=halves_in,
        send_sem=half_sem.at[0],
        recv_sem=half_sem.at[1],
        device_id=sibling,
        device_id_type=MESH,
    )
    swap.start()
    write_own = pltpu.make_async_copy(halves.at[core], vis_out.at[core], out_sem.at[1])
    write_own.start()
    swap.wait_recv()
    write_other = pltpu.make_async_copy(halves_in, vis_out.at[1 - core], out_sem.at[2])
    write_other.start()

    swap.wait_send()
    pair.wait_send()

    @pl.when(ta < 2 * CHIPS - 1)
    def _():
        halo.wait_send()

    def drain(step, carry):
        peer = (col + step) % COLS
        pltpu.make_async_remote_copy(
            src_ref=sendbuf.at[pl.ds(peer * 4, 4)],
            dst_ref=recvbuf.at[col],
            send_sem=a2a_send.at[peer],
            recv_sem=a2a_recv.at[col],
            device_id={"ta": ta, "col": peer},
            device_id_type=MESH,
        ).wait_send()
        return carry

    lax.fori_loop(1, COLS, drain, 0)

    @pl.when(is_end)
    def _():
        for i, j in ORDER:
            if j >= 1:
                stream(outgo_a, from_out, i, j, 0, inner).wait_send()

    @pl.when(is_middle)
    def _():
        for i, j in inward:
            stream(outgo_a, from_in, i, j, 1, inner).wait_send()
        for i, j in outward:
            stream(outgo_b, from_in, i, j, 2, outer).wait_send()

    write_spec.wait()
    write_own.wait()
    write_other.wait()


def body(voltages, taps_filter):
    blocks = (CHIPS * CHIPS, 2, BLK, BLK)
    spectra, visib = pl.pallas_call(
        kernel,
        out_shape=(
            jax.ShapeDtypeStruct((4, FRAMES, NIN), BF16),
            jax.ShapeDtypeStruct((2, 2, 128, NIN), F32),
        ),
        in_specs=[
            pl.BlockSpec(memory_space=pl.ANY),
            pl.BlockSpec(memory_space=pltpu.VMEM),
            pl.BlockSpec(memory_space=pltpu.VMEM),
            pl.BlockSpec(memory_space=pltpu.VMEM),
        ],
        out_specs=(pl.BlockSpec(memory_space=pl.ANY), pl.BlockSpec(memory_space=pl.ANY)),
        scratch_shapes=[
            pltpu.VMEM((FRAMES + TAPS, LOCAL, FR), BF16),
            pltpu.VMEM((JC, FR, FR), BF16),
            pltpu.VMEM((JC * FR, FR), F32),
            pltpu.VMEM((FR, QF, FR), BF16),
            pltpu.VMEM((COLS, 4, QF, FR), BF16),
            pltpu.VMEM((4, FRAMES, NIN), BF16),
            pltpu.VMEM((2, FRAMES, NIN), BF16),
            pltpu.VMEM((4 * FRAMES, NIN), BF16),
            pltpu.VMEM(blocks, F32),
            pltpu.VMEM(blocks, BF16),
            pltpu.VMEM(blocks, BF16),
            pltpu.VMEM(blocks, BF16),
            pltpu.VMEM(blocks, BF16),
            pltpu.VMEM((2, 2, 128, NIN), F32),
            pltpu.VMEM((2, 128, NIN), F32),
            pltpu.SemaphoreType.DMA((1,)),
            pltpu.SemaphoreType.DMA((2,)),
            pltpu.SemaphoreType.DMA((COLS,)),
            pltpu.SemaphoreType.DMA((COLS,)),
            pltpu.SemaphoreType.DMA((1,)),
            pltpu.SemaphoreType.DMA((2,)),
            pltpu.SemaphoreType.DMA((3, CHIPS * CHIPS)),
            pltpu.SemaphoreType.DMA((3, CHIPS * CHIPS)),
            pltpu.SemaphoreType.DMA((2,)),
            pltpu.SemaphoreType.DMA((3,)),
        ],
        compiler_params=pltpu.CompilerParams(
            collective_id=0, has_side_effects=True, vmem_limit_bytes=60 * 2**20
        ),
        name="correlator",
    )(voltages, taps_filter, make_table_rows(), make_regroup())
    return spectra.reshape(2, 2, FRAMES, NIN), jnp.transpose(visib, (2, 0, 1, 3))


def solution(mesh):
    return jax.shard_map(
        body,
        mesh=mesh,
        in_specs=(P("ta", "col", None), P()),
        out_specs=(P("col", None, "ta", None), P("ta", "col", None, None)),
        check_vma=False,
    )
```

time: 258 us -> 122 us (0.47)
  Pallas kernels: 0 us -> 115 us
  waiting for transfers between devices: 85.6 us -> 0 us
  blocking collectives: 67.3 us -> 0 us
  other arithmetic: 44.8 us -> 0 us
  local copies, waits for them, and re-layouts: 23.9 us -> 6 us
  matrix products: 15.1 us -> 0 us
  between operations: 14.1 us -> 0.65 us
  starting transfers between devices: 4.14 us -> 0 us
    pallas_call x0 -> x1, Pallas kernels: none -> 115 us  [body(): pl.pallas_call(kernel, out_shape=(jax.ShapeDtypeStruct((4, FRAMES, NIN),...]
    reduce_scatter x1 -> x0, waiting for transfers between devices: 84.9 us -> none  [body(): lax.psum_scatter(block_gram(turned, turned, scale).astype(jnp.bfloat16),...]
    all_to_all x1 -> x0, blocking collectives: 67.3 us -> none  [body(): lax.all_to_all(spec, 'col', split_axis=0, concat_axis=3, tiled=True)]
    convert_element_type x3 -> x0, other arithmetic: 20.5 us -> none  [the longest x1 9.69 us: body(): block_gram(turned, turned, scale).astype(jnp.bfloat16)]
    dot_general x2 -> x0, matrix products: 15.1 us -> none  [the longest x1 13.1 us: block_gram(): jnp.einsum('cksr,cjsm->ckrjm', left, right, preferred_element_type=jnp.fl...]
    sub x1 -> x0, other arithmetic: 12.2 us -> none  [block_gram(): imag_part = product[:, 0, :, 1] - product[:, 1, :, 0]]
    add x1 -> x0, other arithmetic: 12 us -> none  [block_gram(): real_part = product[:, 0, :, 0] + product[:, 1, :, 1]]
    reshape x1 -> x0, local copies, waits for them, and re-layouts: 8.21 us -> none  [body(): spec = spec.astype(jnp.bfloat16).reshape(frames, local_in, 2, chans)]
  transfers between devices with their start and end apart: 2 -> 0, of which waited for: 2 -> 0; matrix products, arithmetic and copies ran while one was open for 1% -> 0% of each run, Pallas kernels for 0% -> 0%
where the time goes in v1:
time: 122 us; the launch traced here: 121 us
  Pallas kernels  115 us (94%)
  local copies, waits for them, and re-layouts  6 us (5%)
    pallas_call x1, Pallas kernels, body(): pl.pallas_call(kernel, out_shape=(jax.ShapeDtypeStruct((4, FRAMES, NIN),...  115 us
    unnamed x4, local copies, waits for them, and re-layouts  6 us

profile of v1, /device:TPU:33, one launch (start us, length us, event | category | flops | bytes accessed | tf_op | source)
XLA Modules:
  0.0 121.5 jit_solution(13378168522160146167)
XLA Ops:
  0.6 114.8 %correlator.1 = (bf16[4,256,1024]{2,1,0:T(8,128)(2,1)}, f32[2,2,128,1024]{3,2,1,0:T(8,128)}) custom-call(bf16[256,32,128]{2,1,0:T(8,128)(2,1)} %volt.1, f32[16,128]{1,0:T(8,128)} %taps.1, bf16[128,128]{1,0:T(8,128)(2,1)} %constant.6.table, bf16[512,512]{1,0:T(8,128)(2,1)} %constant.5.clone.regroup), custom_call_target="tpu_custom_call" | custom-call | tf_op jit(solution)/shard_map/correlator/pallas_call | solution.py:412
  115.5 0.0 copy-start
  115.5 4.7 %copy.6 = f32[128,2,2,1024]{3,2,1,0:T(2,128)} copy(f32[128,2,2,1024]{3,0,2,1:T(8,128)} %bitcast.3) | data formatting | bytes 4194304
  120.2 0.0 copy-done
  120.2 1.3 %copy.8 = bf16[2,2,256,1024]{3,2,1,0:T(8,128)(2,1)} copy(bf16[2,2,256,1024]{3,2,1,0:T(8,128)(2,1)S(1)} %bitcast.2) | data formatting | bytes 4194304
Async XLA Ops:
  115.5 4.7 %copy-start = (bf16[4,256,1024]{2,1,0:T(8,128)(2,1)S(1)}, bf16[4,256,1024]{2,1,0:T(8,128)(2,1)}, u32[]{:S(2)}) copy-start(bf16[4,256,1024]{2,1,0:T(8,128)(2,1)} %get-tuple-element.4) | copy-start | bytes 6291460

commit v2 on v1

v2 whole, which is shorter than its diff:
```python
import jax
import jax.numpy as jnp
import numpy as np
from jax import lax
from jax.experimental import pallas as pl
from jax.experimental.pallas import tpu as pltpu
from jax.sharding import PartitionSpec as P

MESH = pl.DeviceIdType.MESH
F32 = jnp.float32
BF16 = jnp.bfloat16

TAPS = 16
FR = 128
FRAMES = 256
LOCAL = 32
COLS = 32
NIN = 1024
CHIPS = 4
BLK = NIN // CHIPS
QF = FRAMES // 4
JC = 16
NJC = QF // JC
GROUPS = COLS // 4

ORDER = [(i, j) for j in range(CHIPS - 1, -1, -1) for i in range(j + 1)]


def make_table_rows():
    samples = np.arange(FR)
    chans = np.arange(FR // 2)
    angle = 2.0 * np.pi * ((chans[:, None] * samples[None, :]) % FR) / FR
    both = np.stack([np.cos(angle), -np.sin(angle)], axis=1)
    return jnp.asarray(both.reshape(FR, FR), F32).astype(BF16)


def kernel(
    volt, taps, table, spec_out, vis_out,
    padded, filt, wide, sendbuf, recvbuf, spectra, across, right, for_sibling, part, outgo_a, outgo_b, from_out, from_in, work, stage, arrived, rows_out,
    load_sem, halo_sem, a2a_send, a2a_recv, own_sem, pair_send, pair_recv, line_send, line_recv, half_send, half_recv, out_sem,
):
    ta = lax.axis_index("ta")
    col = lax.axis_index("col")
    chip = ta // 2
    core = ta % 2
    mirror = chip // 2
    middle = chip * (1 - mirror) + (3 - chip) * mirror
    inner = {"ta": (chip + 1 - 2 * mirror) * 2 + core, "col": col}
    outer = {"ta": (chip - 1 + 2 * mirror) * 2 + core, "col": col}
    sibling = {"ta": chip * 2 + 1 - core, "col": col}
    before = {"ta": ta - 1, "col": col}
    after = {"ta": ta + 1, "col": col}
    is_end = middle == 0
    is_middle = middle == 1
    cross_after = jnp.logical_and(core == 1, chip < CHIPS - 1)
    cross_before = jnp.logical_and(core == 0, chip > 0)

    load = pltpu.make_async_copy(volt, padded.at[pl.ds(TAPS, FRAMES)], load_sem.at[0])
    load.start()

    barrier = pltpu.get_barrier_semaphore()

    def greet(device):
        pl.semaphore_signal(barrier, inc=1, device_id=device, device_id_type=MESH)

    def greet_col(step, carry):
        greet({"ta": ta, "col": (col + step) % COLS})
        return carry

    lax.fori_loop(1, COLS, greet_col, 0)
    greet(sibling)
    greet(inner)

    @pl.when(is_middle)
    def _():
        greet(outer)

    @pl.when(cross_after)
    def _():
        greet(after)

    @pl.when(cross_before)
    def _():
        greet(before)

    @pl.when(ta == 0)
    def _():
        padded[0:TAPS] = jnp.zeros((TAPS, LOCAL, FR), BF16)

    load.wait()

    def front(chunk):
        def filter_part(step, carry):
            group = step // 2
            rows = pl.ds(pl.multiple_of((step % 2) * 16, 16), 16)
            out_rows = pl.ds(pl.multiple_of(group * LOCAL + (step % 2) * 16, 16), 16)
            weights = [taps[t : t + 1, :] for t in range(TAPS)]
            for part_of in range(JC // 8):
                base = group * QF + chunk * JC + part_of * 8 + 1
                held = [padded[base + i, rows, :].astype(F32) for i in range(TAPS + 7)]
                for o in range(8):
                    total = weights[0] * held[o]
                    for t in range(1, TAPS):
                        total = total + weights[t] * held[o + t]
                    filt[part_of * 8 + o, out_rows, :] = total.astype(BF16)
            return carry

        lax.fori_loop(0, 8, filter_part, 0)
        for j in range(JC):
            wide[pl.ds(j, FR, stride=JC), :] = lax.dot_general(
                table[...], filt[j], (((1,), (1,)), ((), ())), preferred_element_type=F32
            )
        sendbuf[:, pl.ds(chunk * JC, JC), :] = wide[...].reshape(FR, JC, FR).astype(BF16)

    def to_owner(channel, peer, rows):
        return pltpu.make_async_remote_copy(
            src_ref=sendbuf.at[pl.ds(peer * 4 + 2 * channel, 2), rows],
            dst_ref=recvbuf.at[col, pl.ds(2 * channel, 2), rows],
            send_sem=a2a_send.at[channel, peer],
            recv_sem=a2a_recv.at[channel, col],
            device_id={"ta": ta, "col": peer},
            device_id_type=MESH,
        )

    def send_chunk(channel, rows):
        def send_one(step, carry):
            to_owner(channel, (col + step) % COLS, rows).start()
            return carry

        lax.fori_loop(1, COLS, send_one, 0)

    halo = pltpu.make_async_remote_copy(
        src_ref=padded.at[pl.ds(FRAMES, TAPS)],
        dst_ref=padded.at[pl.ds(0, TAPS)],
        send_sem=halo_sem.at[0],
        recv_sem=halo_sem.at[1],
        device_id=after,
        device_id_type=MESH,
    )

    front(1)
    pl.semaphore_wait(
        barrier,
        COLS + 1 + middle + cross_after.astype(jnp.int32) + cross_before.astype(jnp.int32),
    )

    @pl.when(ta < 2 * CHIPS - 1)
    def _():
        halo.start()

    send_chunk(0, pl.ds(1 * JC, JC))
    front(2)
    send_chunk(0, pl.ds(2 * JC, JC))
    front(3)
    send_chunk(0, pl.ds(3 * JC, JC))

    @pl.when(ta > 0)
    def _():
        halo.wait_recv()

    front(0)
    send_chunk(0, pl.ds(0 * JC, JC))
    send_chunk(1, pl.ds(0, QF))
    own = pltpu.make_async_copy(sendbuf.at[pl.ds(col * 4, 4)], recvbuf.at[col], own_sem.at[0])
    own.start()
    own.wait()

    def pair_copies(channel, lanes):
        own_k, sibling_k = pl.ds(0, 2 * FRAMES), pl.ds(2 * FRAMES, 2 * FRAMES)
        ways = [
            (across.at[channel, lanes, own_k], across.at[channel, lanes, sibling_k]),
            (for_sibling.at[channel, :, lanes], right.at[channel, sibling_k, lanes]),
        ]
        return [
            pltpu.make_async_remote_copy(
                src_ref=src,
                dst_ref=dst,
                send_sem=pair_send.at[channel, way],
                recv_sem=pair_recv.at[channel, way],
                device_id=sibling,
                device_id_type=MESH,
            )
            for way, (src, dst) in enumerate(ways)
        ]

    def gather(channel):
        def regroup_one(g, carry):
            lanes = pl.ds(pl.multiple_of(g * 128, 128), 128)
            for i in range(4):
                source = g * 4 + i

                @pl.when(source != col)
                def _():
                    pltpu.make_async_remote_copy(
                        src_ref=recvbuf.at[source, pl.ds(2 * channel, 2)],
                        dst_ref=recvbuf.at[source, pl.ds(2 * channel, 2)],
                        send_sem=a2a_send.at[channel, source],
                        recv_sem=a2a_recv.at[channel, source],
                        device_id={"ta": ta, "col": source},
                        device_id_type=MESH,
                    ).wait_recv()

            for r in range(2):
                held = [recvbuf[g * 4 + i, 2 * channel + r] for i in range(4)]
                value = jnp.concatenate(
                    [
                        jnp.concatenate([h[:, b * LOCAL : (b + 1) * LOCAL] for h in held], axis=1)
                        for b in range(4)
                    ],
                    axis=0,
                )
                here, there = pl.ds(r * FRAMES, FRAMES), pl.ds((1 - r) * FRAMES, FRAMES)
                spectra[channel, here, lanes] = value
                across[channel, lanes, here] = value.T

                @pl.when(core == 0)
                def _():
                    right[channel, here, lanes] = value
                    for_sibling[channel, there, lanes] = value if r == 1 else -value

                @pl.when(core == 1)
                def _():
                    right[channel, there, lanes] = value if r == 1 else -value
                    for_sibling[channel, here, lanes] = value

            for copy in pair_copies(channel, lanes):
                copy.start()
            return carry

        lax.fori_loop(0, GROUPS, regroup_one, 0)

    def spec_copy(channel):
        return pltpu.make_async_copy(spectra.at[channel], spec_out.at[channel], out_sem.at[channel])

    def actual(i, j):
        return i + mirror * (3 - i - j), j + mirror * (3 - i - j)

    def slot_of(i, j):
        rows, columns = actual(i, j)
        return columns * (columns + 1) // 2 + rows

    def lanes_of(block):
        return pl.ds(pl.multiple_of(block * BLK, BLK), BLK)

    def mine(i, j):
        return None if i != j else core == (i + mirror) % 2

    def if_mine(i, j, run):
        if i == j:
            pl.when(mine(i, j))(run)
        else:
            run()

    def stream(buffer, landing, channel, i, j, way, device):
        slot = slot_of(i, j)
        return pltpu.make_async_remote_copy(
            src_ref=buffer.at[channel, slot],
            dst_ref=landing.at[channel, slot],
            send_sem=line_send.at[channel, way, slot],
            recv_sem=line_recv.at[channel, way, slot],
            device_id=device,
            device_id_type=MESH,
        )


    row_id = lax.broadcasted_iota(jnp.int32, (BLK, BLK), 0)
    col_id = lax.broadcasted_iota(jnp.int32, (BLK, BLK), 1)
    inward = [(i, j) for i, j in ORDER if j >= 2]
    outward = [(0, j) for j in range(CHIPS - 1, -1, -1)]
    forwards = {
        (0, 3): [("in", 0, 3)],
        (1, 3): [("in", 1, 3)],
        (2, 3): [("in", 2, 3)],
        (3, 3): [("in", 3, 3), ("out", 0, 3)],
        (0, 2): [("out", 0, 2)],
        (0, 1): [("out", 0, 1)],
        (0, 0): [("out", 0, 0), ("in", 0, 2), ("in", 1, 2), ("in", 2, 2)],
    }

    def product(channel, i, j):
        rows, columns = actual(i, j)
        slot = slot_of(i, j)
        lhs = across[channel, lanes_of(rows), :]
        value = jnp.dot(lhs, right[channel, :, lanes_of(columns)], preferred_element_type=F32)
        if i == j:
            other = jnp.zeros((BLK, BLK), F32)
            for k in range(4):
                term = jnp.dot(
                    lhs[:, k * FRAMES : (k + 1) * FRAMES],
                    right[channel, (k ^ 1) * FRAMES : ((k ^ 1) + 1) * FRAMES, lanes_of(columns)],
                    preferred_element_type=F32,
                )
                other = other + term if k % 2 == 0 else other - term
            real = jnp.where(core == 0, value, -other)
            imag = jnp.where(core == 0, other, value)
            value = jnp.where(row_id <= col_id, real, imag)
        part[channel, slot] = value
        if j >= 1:

            @pl.when(is_end)
            def _():
                outgo_a[channel, slot] = value.astype(BF16)
                stream(outgo_a, from_out, channel, i, j, 0, inner).start()

    def to_inner(channel, i, j):
        slot = slot_of(i, j)
        stream(outgo_a, from_out, channel, i, j, 0, outer).wait_recv()
        outgo_a[channel, slot] = (part[channel, slot] + from_out[channel, slot].astype(F32)).astype(BF16)
        stream(outgo_a, from_in, channel, i, j, 1, inner).start()

    def to_outer(channel, i, j):
        slot = slot_of(i, j)
        stream(outgo_b, from_in, channel, i, j, 1, inner).wait_recv()
        outgo_b[channel, slot] = (part[channel, slot] + from_in[channel, slot].astype(F32)).astype(BF16)
        stream(outgo_b, from_in, channel, i, j, 2, outer).start()

    def products(channel):
        for i, j in ORDER:
            if_mine(i, j, lambda: product(channel, i, j))

            if (i, j) in forwards:

                @pl.when(is_middle)
                def _():
                    for way, k, l in forwards[i, j]:
                        if_mine(k, l, lambda: (to_inner if way == "in" else to_outer)(channel, k, l))

    scale = 1.0 / (FRAMES * 2 * CHIPS)

    def swap(channel, block, planes):
        return pltpu.make_async_remote_copy(
            src_ref=stage.at[channel, planes, :, lanes_of(block)],
            dst_ref=arrived.at[channel, planes, :, lanes_of(block)],
            send_sem=half_send.at[channel, block],
            recv_sem=half_recv.at[channel, block],
            device_id=sibling,
            device_id_type=MESH,
        )

    def put(channel, block, plane, value):
        rows_out[:, channel, plane, lanes_of(block)] = value

    own_rows = pl.ds(pl.multiple_of(core * 128, 128), 128)
    other_rows = pl.ds(pl.multiple_of((1 - core) * 128, 128), 128)

    def finish_block(channel, i, j, own_is_row, total):
        rows, columns = actual(i, j)
        if i == j:

            @pl.when(mine(i, j))
            def _():
                packed = total() * scale
                flipped = packed.T
                work[0] = jnp.where(row_id <= col_id, packed, flipped)
                work[1] = jnp.where(row_id > col_id, packed, jnp.where(row_id == col_id, 0.0, -flipped))
                for plane in range(2):
                    stage[channel, plane, :, lanes_of(rows)] = work[plane, other_rows, :]
                swap(channel, rows, pl.ds(0, 2)).start()
                for plane in range(2):
                    put(channel, rows, plane, work[plane, own_rows, :])

        else:
            straight = mirror == (0 if own_is_row else 1)
            block = columns * straight.astype(jnp.int32) + rows * (1 - straight.astype(jnp.int32))

            @pl.when(straight)
            def _():
                work[0] = total() * scale

            @pl.when(jnp.logical_not(straight))
            def _():
                work[0] = total().T * (scale * (1 - 2 * core).astype(F32))

            stage[channel, core, :, lanes_of(block)] = work[0, other_rows, :]
            swap(channel, block, pl.ds(core, 1)).start()
            put(channel, block, core, work[0, own_rows, :])

    def finish(channel):
        @pl.when(is_end)
        def _():
            for i, j in outward:
                slot = slot_of(i, j)

                def wait(i=i, j=j):
                    stream(outgo_b, from_in, channel, i, j, 2, inner).wait_recv()

                if_mine(i, j, wait)
                finish_block(
                    channel, i, j, True, lambda: part[channel, slot] + from_in[channel, slot].astype(F32)
                )

        @pl.when(is_middle)
        def _():
            for i, j in [(1, 3), (1, 2), (0, 1), (1, 1)]:
                slot = slot_of(i, j)

                def wait(i=i, j=j):
                    if j == 1:
                        stream(outgo_a, from_out, channel, i, j, 0, outer).wait_recv()
                    if i == 1:
                        stream(outgo_a, from_in, channel, i, j, 1, inner).wait_recv()

                if_mine(i, j, wait)
                finish_block(
                    channel, i, j, i == 1,
                    lambda: part[channel, slot]
                    + from_out[channel, slot].astype(F32)
                    + from_in[channel, slot].astype(F32),
                )

    def collect(channel):
        for block in range(CHIPS):

            @pl.when(chip != block)
            def _():
                swap(channel, block, pl.ds(1 - core, 1)).wait_recv()
                put(channel, block, 1 - core, arrived[channel, 1 - core, :, block * BLK : (block + 1) * BLK])

            @pl.when(jnp.logical_and(chip == block, core != block % 2))
            def _():
                swap(channel, block, pl.ds(0, 2)).wait_recv()
                for plane in range(2):
                    put(channel, block, plane, arrived[channel, plane, :, block * BLK : (block + 1) * BLK])

    def vis_copy(channel):
        return pltpu.make_async_copy(rows_out.at[:, channel], vis_out.at[:, channel], out_sem.at[2 + channel])

    gather(0)
    spec_copy(0).start()
    for copy in pair_copies(0, pl.ds(0, NIN)):
        copy.wait_recv()
    products(0)
    gather(1)
    spec_copy(1).start()
    for copy in pair_copies(1, pl.ds(0, NIN)):
        copy.wait_recv()
    products(1)
    finish(0)
    collect(0)
    vis_copy(0).start()
    finish(1)
    collect(1)
    vis_copy(1).start()

    @pl.when(ta < 2 * CHIPS - 1)
    def _():
        halo.wait_send()

    for channel in range(2):

        def drain(step, carry, channel=channel):
            to_owner(channel, (col + step) % COLS, pl.ds(0, QF)).wait_send()
            return carry

        lax.fori_loop(1, COLS, drain, 0)
        for copy in pair_copies(channel, pl.ds(0, NIN)):
            copy.wait_send()

        @pl.when(is_end)
        def _():
            for i, j in ORDER:
                if j >= 1:
                    if_mine(i, j, lambda: stream(outgo_a, from_out, channel, i, j, 0, inner).wait_send())

        @pl.when(is_middle)
        def _():
            for i, j in inward:
                if_mine(i, j, lambda: stream(outgo_a, from_in, channel, i, j, 1, inner).wait_send())
            for i, j in outward:
                if_mine(i, j, lambda: stream(outgo_b, from_in, channel, i, j, 2, outer).wait_send())

        for block in range(CHIPS):

            @pl.when(chip != block)
            def _():
                swap(channel, block, pl.ds(core, 1)).wait_send()

            @pl.when(jnp.logical_and(chip == block, core == block % 2))
            def _():
                swap(channel, block, pl.ds(0, 2)).wait_send()

        spec_copy(channel).wait()
        vis_copy(channel).wait()


def body(voltages, taps_filter):
    blocks = (2, len(ORDER), BLK, BLK)
    spectra, visib = pl.pallas_call(
        kernel,
        out_shape=(
            jax.ShapeDtypeStruct((2, 2 * FRAMES, NIN), BF16),
            jax.ShapeDtypeStruct((128, 2, 2, NIN), F32),
        ),
        in_specs=[
            pl.BlockSpec(memory_space=pl.ANY),
            pl.BlockSpec(memory_space=pltpu.VMEM),
            pl.BlockSpec(memory_space=pltpu.VMEM),
        ],
        out_specs=(pl.BlockSpec(memory_space=pl.ANY), pl.BlockSpec(memory_space=pl.ANY)),
        scratch_shapes=[
            pltpu.VMEM((FRAMES + TAPS, LOCAL, FR), BF16),
            pltpu.VMEM((JC, FR, FR), BF16),
            pltpu.VMEM((JC * FR, FR), F32),
            pltpu.VMEM((FR, QF, FR), BF16),
            pltpu.VMEM((COLS, 4, QF, FR), BF16),
            pltpu.VMEM((2, 2 * FRAMES, NIN), BF16),
            pltpu.VMEM((2, NIN, 4 * FRAMES), BF16),
            pltpu.VMEM((2, 4 * FRAMES, NIN), BF16),
            pltpu.VMEM((2, 2 * FRAMES, NIN), BF16),
            pltpu.VMEM(blocks, F32),
            pltpu.VMEM(blocks, BF16),
            pltpu.VMEM(blocks, BF16),
            pltpu.VMEM(blocks, BF16),
            pltpu.VMEM(blocks, BF16),
            pltpu.VMEM((2, BLK, BLK), F32),
            pltpu.VMEM((2, 2, 128, NIN), F32),
            pltpu.VMEM((2, 2, 128, NIN), F32),
            pltpu.VMEM((128, 2, 2, NIN), F32),
            pltpu.SemaphoreType.DMA((1,)),
            pltpu.SemaphoreType.DMA((2,)),
            pltpu.SemaphoreType.DMA((2, COLS)),
            pltpu.SemaphoreType.DMA((2, COLS)),
            pltpu.SemaphoreType.DMA((1,)),
            pltpu.SemaphoreType.DMA((2, 2)),
            pltpu.SemaphoreType.DMA((2, 2)),
            pltpu.SemaphoreType.DMA((2, 3, len(ORDER))),
            pltpu.SemaphoreType.DMA((2, 3, len(ORDER))),
            pltpu.SemaphoreType.DMA((2, CHIPS)),
            pltpu.SemaphoreType.DMA((2, CHIPS)),
            pltpu.SemaphoreType.DMA((4,)),
        ],
        compiler_params=pltpu.CompilerParams(
            collective_id=0, has_side_effects=True, vmem_limit_bytes=60 * 2**20
        ),
        name="correlator",
    )(voltages, taps_filter, make_table_rows())
    return spectra.reshape(2, 2, FRAMES, NIN), visib


def solution(mesh):
    return jax.shard_map(
        body,
        mesh=mesh,
        in_specs=(P("ta", "col", None), P()),
        out_specs=(P("col", None, "ta", None), P("ta", "col", None, None)),
        check_vma=False,
    )
```

time: 122 us -> 116 us (0.951)
  Pallas kernels: 115 us -> 110 us
  local copies, waits for them, and re-layouts: 6 us -> 4.55 us
    pallas_call x1, Pallas kernels: 115 us -> 110 us  [body(): pl.pallas_call(kernel, out_shape=(jax.ShapeDtypeStruct((2, 2 * FRAMES, NI...]
    unnamed x4, local copies, waits for them, and re-layouts: 6 us -> 4.55 us
where the time goes in v2:
time: 116 us; the launch traced here: 115 us
  Pallas kernels  110 us (95%)
  local copies, waits for them, and re-layouts  4.55 us (4%)
    pallas_call x1, Pallas kernels, body(): pl.pallas_call(kernel, out_shape=(jax.ShapeDtypeStruct((2, 2 * FRAMES, NI...  110 us
    unnamed x4, local copies, waits for them, and re-layouts  4.55 us

profile of v2, /device:TPU:33, one launch (start us, length us, event | category | flops | bytes accessed | tf_op | source)
XLA Modules:
  0.0 114.7 jit_solution(1181385744783177511)
XLA Ops:
  0.6 109.5 %correlator.1 = (bf16[2,512,1024]{2,1,0:T(8,128)(2,1)}, f32[128,2,2,1024]{3,2,1,0:T(2,128)}) custom-call(bf16[256,32,128]{2,1,0:T(8,128)(2,1)} %volt.1, f32[16,128]{1,0:T(8,128)} %taps.1, bf16[128,128]{1,0:T(8,128)(2,1)} %constant.3.table), custom_call_target="tpu_custom_call" | custom-call | tf_op jit(solution)/shard_map/correlator/pallas_call | solution.py:488
  110.2 0.0 copy-start
  110.2 3.2 %copy.7 = bf16[2,2,256,1024]{3,2,1,0:T(8,128)(2,1)} copy(bf16[2,2,256,1024]{3,2,1,0:T(8,128)(2,1)} %bitcast.1) | data formatting | bytes 4194304
  113.4 0.0 copy-done
  113.4 1.3 %copy.8 = f32[128,2,2,1024]{3,2,1,0:T(2,128)} copy(f32[128,2,2,1024]{3,2,1,0:T(2,128)S(1)} %copy-done) | data formatting | bytes 4194304
Async XLA Ops:
  110.2 3.2 %copy-start = (f32[128,2,2,1024]{3,2,1,0:T(2,128)S(1)}, f32[128,2,2,1024]{3,2,1,0:T(2,128)}, u32[]{:S(2)}) copy-start(f32[128,2,2,1024]{3,2,1,0:T(2,128)} %get-tuple-element.9) | copy-start | bytes 6291460

commit v3 on v2

--- a/solution.py
+++ b/solution.py
@@ -27,16 +27,15 @@
 
 
 def make_table_rows():
-    samples = np.arange(FR)
-    chans = np.arange(FR // 2)
-    angle = 2.0 * np.pi * ((chans[:, None] * samples[None, :]) % FR) / FR
-    both = np.stack([np.cos(angle), -np.sin(angle)], axis=1)
-    return jnp.asarray(both.reshape(FR, FR), F32).astype(BF16)
+    row = lax.broadcasted_iota(jnp.int32, (FR, FR), 0)
+    sample = lax.broadcasted_iota(jnp.int32, (FR, FR), 1)
+    phase = ((row // 2) * sample + (row % 2) * (FR // 4)) % FR
+    return jnp.cos(phase.astype(F32) * (2.0 * np.pi / FR)).astype(BF16)
 
 
 def kernel(
-    volt, taps, table, spec_out, vis_out,
-    padded, filt, wide, sendbuf, recvbuf, spectra, across, right, for_sibling, part, outgo_a, outgo_b, from_out, from_in, work, stage, arrived, rows_out,
+    volt, taps, spec_out, vis_out,
+    table, padded, filt, wide, sendbuf, recvbuf, spectra, across, right, for_sibling, part, outgo_a, outgo_b, from_out, from_in, work, stage, arrived, rows_out,
     load_sem, halo_sem, a2a_send, a2a_recv, own_sem, pair_send, pair_recv, line_send, line_recv, half_send, half_recv, out_sem,
 ):
     ta = lax.axis_index("ta")
@@ -55,8 +54,19 @@
     cross_after = jnp.logical_and(core == 1, chip < CHIPS - 1)
     cross_before = jnp.logical_and(core == 0, chip > 0)
 
-    load = pltpu.make_async_copy(volt, padded.at[pl.ds(TAPS, FRAMES)], load_sem.at[0])
-    load.start()
+    def loads(half):
+        return [
+            pltpu.make_async_copy(
+                volt.at[pl.ds(b * QF + half * (QF // 2), QF // 2)],
+                padded.at[pl.ds(TAPS + b * QF + half * (QF // 2), QF // 2)],
+                load_sem.at[half, b],
+            )
+            for b in range(4)
+        ]
+
+    for half in range(2):
+        for load in loads(half):
+            load.start()
 
     barrier = pltpu.get_barrier_semaphore()
 
@@ -87,7 +97,9 @@
     def _():
         padded[0:TAPS] = jnp.zeros((TAPS, LOCAL, FR), BF16)
 
-    load.wait()
+    table[...] = make_table_rows()
+    for load in loads(0):
+        load.wait()
 
     def front(chunk):
         def filter_part(step, carry):
@@ -139,6 +151,8 @@
     )
 
     front(1)
+    for load in loads(1):
+        load.wait()
     pl.semaphore_wait(
         barrier,
         COLS + 1 + middle + cross_after.astype(jnp.int32) + cross_before.astype(jnp.int32),
@@ -163,7 +177,6 @@
     send_chunk(1, pl.ds(0, QF))
     own = pltpu.make_async_copy(sendbuf.at[pl.ds(col * 4, 4)], recvbuf.at[col], own_sem.at[0])
     own.start()
-    own.wait()
 
     def pair_copies(channel, lanes):
         own_k, sibling_k = pl.ds(0, 2 * FRAMES), pl.ds(2 * FRAMES, 2 * FRAMES)
@@ -242,12 +255,12 @@
     def lanes_of(block):
         return pl.ds(pl.multiple_of(block * BLK, BLK), BLK)
 
-    def mine(i, j):
-        return None if i != j else core == (i + mirror) % 2
-
-    def if_mine(i, j, run):
+    def mine(channel, i, j):
+        return None if i != j else core == (i + mirror + channel) % 2
+
+    def if_mine(channel, i, j, run):
         if i == j:
-            pl.when(mine(i, j))(run)
+            pl.when(mine(channel, i, j))(run)
         else:
             run()
 
@@ -316,14 +329,14 @@
 
     def products(channel):
         for i, j in ORDER:
-            if_mine(i, j, lambda: product(channel, i, j))
+            if_mine(channel, i, j, lambda: product(channel, i, j))
 
             if (i, j) in forwards:
 
                 @pl.when(is_middle)
                 def _():
                     for way, k, l in forwards[i, j]:
-                        if_mine(k, l, lambda: (to_inner if way == "in" else to_outer)(channel, k, l))
+                        if_mine(channel, k, l, lambda: (to_inner if way == "in" else to_outer)(channel, k, l))
 
     scale = 1.0 / (FRAMES * 2 * CHIPS)
 
@@ -347,7 +360,7 @@
         rows, columns = actual(i, j)
         if i == j:
 
-            @pl.when(mine(i, j))
+            @pl.when(mine(channel, i, j))
             def _():
                 packed = total() * scale
                 flipped = packed.T
@@ -384,7 +397,7 @@
                 def wait(i=i, j=j):
                     stream(outgo_b, from_in, channel, i, j, 2, inner).wait_recv()
 
-                if_mine(i, j, wait)
+                if_mine(channel, i, j, wait)
                 finish_block(
                     channel, i, j, True, lambda: part[channel, slot] + from_in[channel, slot].astype(F32)
                 )
@@ -400,7 +413,7 @@
                     if i == 1:
                         stream(outgo_a, from_in, channel, i, j, 1, inner).wait_recv()
 
-                if_mine(i, j, wait)
+                if_mine(channel, i, j, wait)
                 finish_block(
                     channel, i, j, i == 1,
                     lambda: part[channel, slot]
@@ -408,23 +421,32 @@
                     + from_in[channel, slot].astype(F32),
                 )
 
+    def block_copy(channel, block):
+        lanes = lanes_of(block)
+        return pltpu.make_async_copy(
+            rows_out.at[:, channel, :, lanes], vis_out.at[:, channel, :, lanes], out_sem.at[2 + channel]
+        )
+
     def collect(channel):
-        for block in range(CHIPS):
-
-            @pl.when(chip != block)
-            def _():
+        for place in (3, 2, 1 - middle, middle):
+            block = place + mirror * (3 - 2 * place)
+            if place is not middle:
                 swap(channel, block, pl.ds(1 - core, 1)).wait_recv()
-                put(channel, block, 1 - core, arrived[channel, 1 - core, :, block * BLK : (block + 1) * BLK])
-
-            @pl.when(jnp.logical_and(chip == block, core != block % 2))
-            def _():
-                swap(channel, block, pl.ds(0, 2)).wait_recv()
-                for plane in range(2):
-                    put(channel, block, plane, arrived[channel, plane, :, block * BLK : (block + 1) * BLK])
+                put(channel, block, 1 - core, arrived[channel, 1 - core, :, lanes_of(block)])
+            else:
+
+                @pl.when(core != (block + channel) % 2)
+                def _():
+                    swap(channel, block, pl.ds(0, 2)).wait_recv()
+                    for plane in range(2):
+                        put(channel, block, plane, arrived[channel, plane, :, lanes_of(block)])
+
+            block_copy(channel, block).start()
 
     def vis_copy(channel):
         return pltpu.make_async_copy(rows_out.at[:, channel], vis_out.at[:, channel], out_sem.at[2 + channel])
 
+    own.wait()
     gather(0)
     spec_copy(0).start()
     for copy in pair_copies(0, pl.ds(0, NIN)):
@@ -437,10 +459,8 @@
     products(1)
     finish(0)
     collect(0)
-    vis_copy(0).start()
     finish(1)
     collect(1)
-    vis_copy(1).start()
 
     @pl.when(ta < 2 * CHIPS - 1)
     def _():
@@ -460,14 +480,14 @@
         def _():
             for i, j in ORDER:
                 if j >= 1:
-                    if_mine(i, j, lambda: stream(outgo_a, from_out, channel, i, j, 0, inner).wait_send())
+                    if_mine(channel, i, j, lambda: stream(outgo_a, from_out, channel, i, j, 0, inner).wait_send())
 
         @pl.when(is_middle)
         def _():
             for i, j in inward:
-                if_mine(i, j, lambda: stream(outgo_a, from_in, channel, i, j, 1, inner).wait_send())
+                if_mine(channel, i, j, lambda: stream(outgo_a, from_in, channel, i, j, 1, inner).wait_send())
             for i, j in outward:
-                if_mine(i, j, lambda: stream(outgo_b, from_in, channel, i, j, 2, outer).wait_send())
+                if_mine(channel, i, j, lambda: stream(outgo_b, from_in, channel, i, j, 2, outer).wait_send())
 
         for block in range(CHIPS):
 
@@ -475,7 +495,7 @@
             def _():
                 swap(channel, block, pl.ds(core, 1)).wait_send()
 
-            @pl.when(jnp.logical_and(chip == block, core == block % 2))
+            @pl.when(jnp.logical_and(chip == block, core == (block + channel) % 2))
             def _():
                 swap(channel, block, pl.ds(0, 2)).wait_send()
 
@@ -494,10 +514,10 @@
         in_specs=[
             pl.BlockSpec(memory_space=pl.ANY),
             pl.BlockSpec(memory_space=pltpu.VMEM),
-            pl.BlockSpec(memory_space=pltpu.VMEM),
         ],
         out_specs=(pl.BlockSpec(memory_space=pl.ANY), pl.BlockSpec(memory_space=pl.ANY)),
         scratch_shapes=[
+            pltpu.VMEM((FR, FR), BF16),
             pltpu.VMEM((FRAMES + TAPS, LOCAL, FR), BF16),
             pltpu.VMEM((JC, FR, FR), BF16),
             pltpu.VMEM((JC * FR, FR), F32),
@@ -516,7 +536,7 @@
             pltpu.VMEM((2, 2, 128, NIN), F32),
             pltpu.VMEM((2, 2, 128, NIN), F32),
             pltpu.VMEM((128, 2, 2, NIN), F32),
-            pltpu.SemaphoreType.DMA((1,)),
+            pltpu.SemaphoreType.DMA((2, 4)),
             pltpu.SemaphoreType.DMA((2,)),
             pltpu.SemaphoreType.DMA((2, COLS)),
             pltpu.SemaphoreType.DMA((2, COLS)),
@@ -530,10 +550,10 @@
             pltpu.SemaphoreType.DMA((4,)),
         ],
         compiler_params=pltpu.CompilerParams(
-            collective_id=0, has_side_effects=True, vmem_limit_bytes=60 * 2**20
+            collective_id=0, has_side_effects=True, vmem_limit_bytes=48 * 2**20
         ),
         name="correlator",
-    )(voltages, taps_filter, make_table_rows())
+    )(voltages, taps_filter)
     return spectra.reshape(2, 2, FRAMES, NIN), visib
 
 

time: 116 us -> 113 us (0.974); the launches traced: 115 us -> 113 us
  local copies, waits for them, and re-layouts: 4.55 us -> 3.33 us
    unnamed x4, local copies, waits for them, and re-layouts: 4.55 us -> 3.33 us
where the time goes in v3:
time: 113 us
  Pallas kernels  109 us (96%)
  local copies, waits for them, and re-layouts  3.33 us (3%)
    pallas_call x1, Pallas kernels, body(): pl.pallas_call(kernel, out_shape=(jax.ShapeDtypeStruct((2, 2 * FRAMES, NI...  109 us
    unnamed x4, local copies, waits for them, and re-layouts  3.33 us

profile of v3, /device:TPU:33, one launch (start us, length us, event | category | flops | bytes accessed | tf_op | source)
XLA Modules:
  0.0 113.1 jit_solution(5643221703681864633)
XLA Ops:
  0.6 0.0 copy-start
  0.6 0.7 copy-done
  1.3 109.1 %correlator.1 = (bf16[2,512,1024]{2,1,0:T(8,128)(2,1)S(1)}, f32[128,2,2,1024]{3,2,1,0:T(2,128)S(1)}) custom-call(bf16[256,32,128]{2,1,0:T(8,128)(2,1)} %volt.1, f32[16,128]{1,0:T(8,128)S(1)} %copy-done), custom_call_target="tpu_custom_call" | custom-call | tf_op jit(solution)/shard_map/correlator/pallas_call | solution.py:508
  110.5 1.3 %copy.6 = bf16[2,2,256,1024]{3,2,1,0:T(8,128)(2,1)} copy(bf16[2,2,256,1024]{3,2,1,0:T(8,128)(2,1)S(1)} %bitcast.1) | data formatting | bytes 4194304
  111.8 1.3 %copy.7 = f32[128,2,2,1024]{3,2,1,0:T(2,128)} copy(f32[128,2,2,1024]{3,2,1,0:T(2,128)S(1)} %get-tuple-element.9) | data formatting | bytes 4194304
Async XLA Ops:
  0.6 0.7 copy-start

commit v4 on v3

--- a/solution.py
+++ b/solution.py
@@ -23,7 +23,7 @@
 NJC = QF // JC
 GROUPS = COLS // 4
 
-ORDER = [(i, j) for j in range(CHIPS - 1, -1, -1) for i in range(j + 1)]
+ORDER = [(0, 3), (1, 3), (2, 3), (3, 3), (0, 2), (1, 2), (2, 2), (1, 1), (0, 1), (0, 0)]
 
 
 def make_table_rows():
@@ -313,7 +313,8 @@
             @pl.when(is_end)
             def _():
                 outgo_a[channel, slot] = value.astype(BF16)
-                stream(outgo_a, from_out, channel, i, j, 0, inner).start()
+                if j >= 2 or channel == 1:
+                    stream(outgo_a, from_out, channel, i, j, 0, inner).start()
 
     def to_inner(channel, i, j):
         slot = slot_of(i, j)
@@ -330,6 +331,14 @@
     def products(channel):
         for i, j in ORDER:
             if_mine(channel, i, j, lambda: product(channel, i, j))
+
+            if (i, j) == (2, 2) and channel == 1:
+
+                @pl.when(is_end)
+                def _():
+                    for k, l in [(1, 1), (0, 1)]:
+                        if_mine(0, k, l, lambda: stream(outgo_a, from_out, 0, k, l, 0, inner).start())
+
 
             if (i, j) in forwards:
 
@@ -404,7 +413,7 @@
 
         @pl.when(is_middle)
         def _():
-            for i, j in [(1, 3), (1, 2), (0, 1), (1, 1)]:
+            for i, j in [(1, 3), (1, 2), (1, 1), (0, 1)]:
                 slot = slot_of(i, j)
 
                 def wait(i=i, j=j):
@@ -428,23 +437,64 @@
         )
 
     def collect(channel):
-        for place in (3, 2, 1 - middle, middle):
+        for place in (3, 2, 1, 0):
             block = place + mirror * (3 - 2 * place)
-            if place is not middle:
+
+            @pl.when(middle != place)
+            def _():
                 swap(channel, block, pl.ds(1 - core, 1)).wait_recv()
                 put(channel, block, 1 - core, arrived[channel, 1 - core, :, lanes_of(block)])
-            else:
-
-                @pl.when(core != (block + channel) % 2)
-                def _():
-                    swap(channel, block, pl.ds(0, 2)).wait_recv()
-                    for plane in range(2):
-                        put(channel, block, plane, arrived[channel, plane, :, lanes_of(block)])
+
+            @pl.when(jnp.logical_and(middle == place, core != (block + channel) % 2))
+            def _():
+                swap(channel, block, pl.ds(0, 2)).wait_recv()
+                for plane in range(2):
+                    put(channel, block, plane, arrived[channel, plane, :, lanes_of(block)])
 
             block_copy(channel, block).start()
 
     def vis_copy(channel):
         return pltpu.make_async_copy(rows_out.at[:, channel], vis_out.at[:, channel], out_sem.at[2 + channel])
+
+    def drain_spectra():
+        @pl.when(ta < 2 * CHIPS - 1)
+        def _():
+            halo.wait_send()
+
+        for channel in range(2):
+
+            def drain(step, carry, channel=channel):
+                to_owner(channel, (col + step) % COLS, pl.ds(0, QF)).wait_send()
+                return carry
+
+            lax.fori_loop(1, COLS, drain, 0)
+            for copy in pair_copies(channel, pl.ds(0, NIN)):
+                copy.wait_send()
+            spec_copy(channel).wait()
+
+    def drain_line(channel):
+        @pl.when(is_end)
+        def _():
+            for i, j in ORDER:
+                if j >= 1:
+                    if_mine(channel, i, j, lambda: stream(outgo_a, from_out, channel, i, j, 0, inner).wait_send())
+
+        @pl.when(is_middle)
+        def _():
+            for i, j in inward:
+                if_mine(channel, i, j, lambda: stream(outgo_a, from_in, channel, i, j, 1, inner).wait_send())
+            for i, j in outward:
+                if_mine(channel, i, j, lambda: stream(outgo_b, from_in, channel, i, j, 2, outer).wait_send())
+
+        for block in range(CHIPS):
+
+            @pl.when(chip != block)
+            def _():
+                swap(channel, block, pl.ds(core, 1)).wait_send()
+
+            @pl.when(jnp.logical_and(chip == block, core == (block + channel) % 2))
+            def _():
+                swap(channel, block, pl.ds(0, 2)).wait_send()
 
     own.wait()
     gather(0)
@@ -459,48 +509,13 @@
     products(1)
     finish(0)
     collect(0)
+    drain_spectra()
+    drain_line(0)
     finish(1)
     collect(1)
-
-    @pl.when(ta < 2 * CHIPS - 1)
-    def _():
-        halo.wait_send()
-
-    for channel in range(2):
-
-        def drain(step, carry, channel=channel):
-            to_owner(channel, (col + step) % COLS, pl.ds(0, QF)).wait_send()
-            return carry
-
-        lax.fori_loop(1, COLS, drain, 0)
-        for copy in pair_copies(channel, pl.ds(0, NIN)):
-            copy.wait_send()
-
-        @pl.when(is_end)
-        def _():
-            for i, j in ORDER:
-                if j >= 1:
-                    if_mine(channel, i, j, lambda: stream(outgo_a, from_out, channel, i, j, 0, inner).wait_send())
-
-        @pl.when(is_middle)
-        def _():
-            for i, j in inward:
-                if_mine(channel, i, j, lambda: stream(outgo_a, from_in, channel, i, j, 1, inner).wait_send())
-            for i, j in outward:
-                if_mine(channel, i, j, lambda: stream(outgo_b, from_in, channel, i, j, 2, outer).wait_send())
-
-        for block in range(CHIPS):
-
-            @pl.when(chip != block)
-            def _():
-                swap(channel, block, pl.ds(core, 1)).wait_send()
-
-            @pl.when(jnp.logical_and(chip == block, core == (block + channel) % 2))
-            def _():
-                swap(channel, block, pl.ds(0, 2)).wait_send()
-
-        spec_copy(channel).wait()
-        vis_copy(channel).wait()
+    drain_line(1)
+    vis_copy(0).wait()
+    vis_copy(1).wait()
 
 
 def body(voltages, taps_filter):

time: 113 us -> 111 us (0.982)
  Pallas kernels: 109 us -> 107 us
    pallas_call x1, Pallas kernels: 109 us -> 107 us  [body(): pl.pallas_call(kernel, out_shape=(jax.ShapeDtypeStruct((2, 2 * FRAMES, NI...]
where the time goes in v4:
time: 111 us
  Pallas kernels  107 us (96%)
  local copies, waits for them, and re-layouts  3.33 us (3%)
    pallas_call x1, Pallas kernels, body(): pl.pallas_call(kernel, out_shape=(jax.ShapeDtypeStruct((2, 2 * FRAMES, NI...  107 us
    unnamed x4, local copies, waits for them, and re-layouts  3.33 us

profile of v4, /device:TPU:33, one launch (start us, length us, event | category | flops | bytes accessed | tf_op | source)
XLA Modules:
  0.0 110.7 jit_solution(12096522661708195183)
XLA Ops:
  0.6 0.0 copy-start
  0.6 0.7 copy-done
  1.3 106.7 %correlator.1 = (bf16[2,512,1024]{2,1,0:T(8,128)(2,1)S(1)}, f32[128,2,2,1024]{3,2,1,0:T(2,128)S(1)}) custom-call(bf16[256,32,128]{2,1,0:T(8,128)(2,1)} %volt.1, f32[16,128]{1,0:T(8,128)S(1)} %copy-done), custom_call_target="tpu_custom_call" | custom-call | tf_op jit(solution)/shard_map/correlator/pallas_call | solution.py:523
  108.1 1.3 %copy.6 = bf16[2,2,256,1024]{3,2,1,0:T(8,128)(2,1)} copy(bf16[2,2,256,1024]{3,2,1,0:T(8,128)(2,1)S(1)} %bitcast.1) | data formatting | bytes 4194304
  109.4 1.3 %copy.7 = f32[128,2,2,1024]{3,2,1,0:T(2,128)} copy(f32[128,2,2,1024]{3,2,1,0:T(2,128)S(1)} %get-tuple-element.9) | data formatting | bytes 4194304
Async XLA Ops:
  0.6 0.7 copy-start

commit v5 on v4

--- a/solution.py
+++ b/solution.py
@@ -472,19 +472,20 @@
                 copy.wait_send()
             spec_copy(channel).wait()
 
+    def drain_middle(channel):
+        @pl.when(is_middle)
+        def _():
+            for i, j in inward:
+                if_mine(channel, i, j, lambda: stream(outgo_a, from_in, channel, i, j, 1, inner).wait_send())
+            for i, j in outward:
+                if_mine(channel, i, j, lambda: stream(outgo_b, from_in, channel, i, j, 2, outer).wait_send())
+
     def drain_line(channel):
         @pl.when(is_end)
         def _():
             for i, j in ORDER:
                 if j >= 1:
                     if_mine(channel, i, j, lambda: stream(outgo_a, from_out, channel, i, j, 0, inner).wait_send())
-
-        @pl.when(is_middle)
-        def _():
-            for i, j in inward:
-                if_mine(channel, i, j, lambda: stream(outgo_a, from_in, channel, i, j, 1, inner).wait_send())
-            for i, j in outward:
-                if_mine(channel, i, j, lambda: stream(outgo_b, from_in, channel, i, j, 2, outer).wait_send())
 
         for block in range(CHIPS):
 
@@ -511,6 +512,8 @@
     collect(0)
     drain_spectra()
     drain_line(0)
+    drain_middle(0)
+    drain_middle(1)
     finish(1)
     collect(1)
     drain_line(1)

time: 111 us -> 111 us (level)
  no operation moved by 1% of the time
where the time goes in v5:
time: 111 us
  Pallas kernels  107 us (96%)
  local copies, waits for them, and re-layouts  3.33 us (3%)
    pallas_call x1, Pallas kernels, body(): pl.pallas_call(kernel, out_shape=(jax.ShapeDtypeStruct((2, 2 * FRAMES, NI...  107 us
    unnamed x4, local copies, waits for them, and re-layouts  3.33 us

profile of v5, /device:TPU:33, one launch (start us, length us, event | category | flops | bytes accessed | tf_op | source)
XLA Modules:
  0.0 110.7 jit_solution(185975820613929769)
XLA Ops:
  0.6 0.0 copy-start
  0.6 0.7 copy-done
  1.3 106.7 %correlator.1 = (bf16[2,512,1024]{2,1,0:T(8,128)(2,1)S(1)}, f32[128,2,2,1024]{3,2,1,0:T(2,128)S(1)}) custom-call(bf16[256,32,128]{2,1,0:T(8,128)(2,1)} %volt.1, f32[16,128]{1,0:T(8,128)S(1)} %copy-done), custom_call_target="tpu_custom_call" | custom-call | tf_op jit(solution)/shard_map/correlator/pallas_call | solution.py:526
  108.1 1.3 %copy.6 = bf16[2,2,256,1024]{3,2,1,0:T(8,128)(2,1)} copy(bf16[2,2,256,1024]{3,2,1,0:T(8,128)(2,1)S(1)} %bitcast.1) | data formatting | bytes 4194304
  109.4 1.3 %copy.7 = f32[128,2,2,1024]{3,2,1,0:T(2,128)} copy(f32[128,2,2,1024]{3,2,1,0:T(2,128)S(1)} %get-tuple-element.9) | data formatting | bytes 4194304
Async XLA Ops:
  0.6 0.7 copy-start
